TPU v7x, 256 devices: a whole 4x4x8 slice. The times are simulated.
256 devices in a mesh: pipe: 8 (over z), section: 4 (over y_hi, core), tensor: 8 (over x, y_lo).
Axes of the slice: x: 4, y: 4 (y_hi: 2, y_lo: 2; y = y_hi * 2 + y_lo), z: 8, core: 2. Of those that a mesh axis runs over, the one named last changes fastest.
Arguments:
- tokens: bfloat16 [8, 4, 2, 256, 8192], P('pipe', 'section', None, None, 'tensor'), may hold values from -51 to 51
- norm_gain: bfloat16 [4, 8192], P('section', 'tensor'), may hold values from 0.25 to 1.75
- held_kv: bfloat16 [4, 8192, 2048], P('section', 'tensor', 'pipe'), may hold values from -0.0625 to 0.0625
- block_holder: int32 [4, 8], replicated, may hold values from 0 to 7, each once within a row
- section_layer: int32 [8, 4], replicated, may hold values from 0 to 3, each once within a row
- cotangent: bfloat16 [8, 4, 2, 256, 2048], P('pipe', 'section', None, None, 'tensor'), may hold values from -6 to 6
Outputs:
- keys_values: bfloat16 [8, 4, 2, 256, 2048], P('pipe', 'section', None, None, 'tensor')
- token_grad: bfloat16 [8, 4, 2, 256, 8192], P('pipe', 'section', None, None, 'tensor')
- kv_grads: bfloat16 [4, 8192, 2048], P('section', 'tensor', 'pipe')
Inputs may be any that keep to these rules, and one draw needn't show every extreme that they name: Each row of section_layer is a permutation of the 4 window layers. Each row of block_holder is a permutation of the 8 relays.
All inputs are finite; a program needn't handle non-finite values.
Results may differ from a plain program's by a relative error of at most 0.0057.
Values may be sent and summed in bfloat16 or wider, within the bound.
No kernel may reach another device: no remote copies, remote signals or barrier semaphores. Data moves between devices by JAX's collectives and lax.ppermute only.
A program may use at most 128 MiB of HBM per device.

v0:
```python
import jax
import jax.numpy as jnp
from jax import lax
from jax.sharding import PartitionSpec as P

D = 8192
EPSILON = 1e-05


def invert_slots(holder_row):
    slot_count = holder_row.shape[0]
    slot_ids = jnp.arange(slot_count, dtype=jnp.int32)
    slot_match = holder_row[None, :] == slot_ids[:, None]
    return jnp.sum(jnp.where(slot_match, slot_ids[None, :], 0), axis=1)


def per_device(tokens, norm_gain, held_kv, block_holder, section_layer, cotangent):
    pipe_index = lax.axis_index("pipe")
    section_index = lax.axis_index("section")
    pipe_count = lax.axis_size("pipe")
    section_count = lax.axis_size("section")
    layer_index = section_layer[pipe_index, section_index]
    every_block, every_gain = (
        lax.all_gather(held_kv, ("pipe", "section"), axis=0, tiled=True),
        lax.all_gather(norm_gain, ("pipe", "section"), axis=0, tiled=True),
    )
    sources = jnp.arange(pipe_count, dtype=jnp.int32) * section_count + layer_index
    my_blocks = jnp.take(every_block, sources, axis=0)
    layer_gain = every_gain[layer_index]
    weight_blocks = jnp.take(my_blocks, block_holder[layer_index], axis=0)
    gain_f32 = layer_gain.astype(jnp.float32)
    micro_count = tokens.shape[2]
    tok_count = tokens.shape[3]
    feat_local = tokens.shape[4]
    row_count = micro_count * tok_count
    inputs = tokens.reshape(row_count, feat_local).astype(jnp.float32)
    squares = lax.psum(jnp.sum(inputs * inputs, axis=1), "tensor")
    scale_rows = lax.rsqrt(squares / D + EPSILON)
    normed = (inputs * scale_rows[:, None] * gain_f32).astype(jnp.bfloat16)
    partial_kv = jnp.einsum(
        "rd,bdc->rbc", normed, weight_blocks, preferred_element_type=jnp.float32
    ).reshape(row_count, -1)
    kv_local = lax.psum_scatter(partial_kv, "tensor", scatter_dimension=1, tiled=True)
    keys_values = kv_local.astype(jnp.bfloat16).reshape(1, 1, micro_count, tok_count, -1)
    upstream_local = cotangent.reshape(row_count, -1)
    upstream = lax.all_gather(upstream_local, "tensor", axis=1, tiled=True)
    upstream_blocks = upstream.reshape(row_count, pipe_count, -1)
    normed_grad = jnp.einsum(
        "rbc,bdc->rd", upstream_blocks, weight_blocks, preferred_element_type=jnp.float32
    )
    grad_blocks = jnp.einsum(
        "rd,rbc->bdc", normed, upstream_blocks, preferred_element_type=jnp.float32
    ).astype(jnp.bfloat16)
    outgoing_grads = jnp.take(grad_blocks, invert_slots(block_holder[layer_index]), axis=0)
    arrived = lax.all_to_all(outgoing_grads, "pipe", split_axis=0, concat_axis=0, tiled=True)
    layer_ids = jnp.arange(section_count, dtype=jnp.int32)
    owner_table = (section_layer[:, section_index][None, :] == layer_ids[:, None]).astype(
        jnp.bfloat16
    )
    per_layer = jnp.einsum("lq,qdc->ldc", owner_table, arrived, preferred_element_type=jnp.float32)
    summed = lax.psum_scatter(per_layer, "section", scatter_dimension=0, tiled=True)
    kv_grads = summed.astype(jnp.bfloat16)
    row_inner = lax.psum(jnp.sum(gain_f32 * normed_grad * inputs, axis=1), "tensor")
    token_grad = (
        scale_rows[:, None] * gain_f32 * normed_grad
        - inputs * (scale_rows**3 * row_inner / D)[:, None]
    ).astype(jnp.bfloat16)
    return (keys_values, token_grad.reshape(tokens.shape), kv_grads)


def solution(mesh):
    placed = (
        P("pipe", "section", None, None, "tensor"),
        P("section", "tensor"),
        P("section", "tensor", "pipe"),
        P(),
        P(),
        P("pipe", "section", None, None, "tensor"),
    )
    return jax.shard_map(
        per_device,
        mesh=mesh,
        in_specs=placed,
        out_specs=(
            P("pipe", "section", None, None, "tensor"),
            P("pipe", "section", None, None, "tensor"),
            P("section", "tensor", "pipe"),
        ),
        check_vma=False,
    )
```

profile of v0, /device:TPU:1, one launch (start us, length us, event | category | flops | bytes accessed | tf_op | source)
XLA Modules:
  0.0 425.6 jit_solution(6199539240854835074)
XLA Ops:
  7.2 0.7 all-gather.4.cloned.1.call-update
  7.9 1.8 copy.39
  9.8 1.3 dynamic_slice.13
  14.3 1.5 fusion.6
  15.8 46.9 %all-gather = bf16[32,1,1024]{2,1,0:T(2,128)(2,1)S(1)} all-gather(bf16[1,1,1024]{2,1,0:T(2,128)(2,1)} %bitcast.61), channel_id=1, replica_groups=mesh['pipe'=8,'section'=4,'tensor'=8] {'pipe','section'}, dimensions={0}, use_global_device_ids=true | all-gather | bytes 67584 | tf_op jit(solution)/shard_map/all_gather | solution.py:25
  62.8 0.7 fusion.18
  63.4 0.7 compare_and_fusion.2
  64.1 0.7 compare_and_fusion.1
  65.0 87.9 %all-gather.4.cloned.1.call-done = bf16[32,1024,256]{2,1,0:T(8,128)(2,1)} async-done(((bf16[1,1024,256]{2,1,0:T(8,128)(2,1)}), bf16[32,1024,256]{2,1,0:T(8,128)(2,1)}) %all-gather.4.cloned.1.call-update) | async-done | bytes 16777232 | tf_op jit(solution)/shard_map/all_gather | solution.py:24
  152.9 8.5 %gather_fusion = bf16[8,1024,256]{2,1,0:T(8,128)(2,1)} fusion(bf16[32,1024,256]{2,1,0:T(8,128)(2,1)} %all-gather.4.cloned.1.call-done, s32[1024]{0:T(1024)S(1)} %pad_clamp_fusion.2), kind=kCustom, calls=%fused_computation.2 | custom fusion | bytes 8388640 | tf_op jit(solution)/shard_map/jit(_take)/gather | solution.py:28
  161.4 4.7 %broadcast_select_fusion.2 = bf16[8,1024,256]{2,1,0:T(8,128)(2,1)} fusion(bf16[8,1024,256]{2,1,0:T(8,128)(2,1)} %gather_fusion, pred[8]{0:T(512)(128)(4,1)S(1)} %compare_and_fusion.2), kind=kLoop, calls=%fused_computation.8 | loop fusion | flops 2097152 | bytes 8388616 | tf_op jit(solution)/shard_map/jit(_take)/select_n | solution.py:28
  166.1 4.9 %gather_fusion.1 = bf16[8,1024,256]{2,1,0:T(8,128)(2,1)} fusion(bf16[8,1024,256]{2,1,0:T(8,128)(2,1)} %broadcast_select_fusion.2, s32[1024]{0:T(1024)S(1)} %pad_clamp_fusion.1), kind=kCustom, calls=%fused_computation.clone | custom fusion | bytes 8388640 | tf_op jit(solution)/shard_map/jit(_take)/gather | solution.py:30
  171.0 4.7 %fusion.10 = bf16[8,256,1024]{1,2,0:T(8,128)(2,1)} fusion(bf16[8,1024,256]{2,1,0:T(8,128)(2,1)} %gather_fusion.1, pred[8]{0:T(512)(128)(4,1)S(1)} %get-tuple-element.15), kind=kLoop, calls=%fused_computation.22 | loop fusion | flops 2097152 | bytes 8388616 | tf_op jit(solution)/shard_map/rd,bdc->rbc/dot_general | solution.py:40
  175.7 28.8 %all-gather.6.cloned.1.call-done = bf16[512,2048]{0,1:T(8,128)(2,1)} async-done(((bf16[512,256]{0,1:T(8,128)(2,1)}), bf16[512,2048]{0,1:T(8,128)(2,1)}) %all-gather.6.cloned.1.call-update) | async-done | bytes 2097168 | tf_op jit(solution)/shard_map/all_gather | solution.py:46
  204.5 5.4 %fusion.5 = (f32[512]{0:T(512)S(1)}, f32[1024,512,1]{0,1,2:T(8,128)S(1)}) fusion(bf16[1,1,2,256,1024]{4,3,2,1,0:T(8,128)(2,1)S(1)} %copy-done, f32[1024]{0:T(1024)S(1)} %bitcast.56, bf16[512,8,256]{0,2,1:T(8,128)(2,1)} %bitcast.62, bf16[8,1024,256]{2,1,0:T(8,128)(2,1)} %gather_fusion.1, pred[8]{0:T(512)(128)(4,1)S(1)} %get-tuple-element.15), kind=kOutput, calls=%fused_computation.14 | convolution fusion | flops 2151677440 | bytes 9443336 | tf_op jit(solution)/shard_map/rbc,bdc->rd/dot_general | solution.py:48
  209.9 14.6 %all-reduce = (f32[512]{0:T(512)S(1)}, f32[512]{0:T(512)S(1)}) all-reduce(f32[512]{0:T(512)S(1)} %bitcast.60, f32[512]{0:T(512)S(1)} %get-tuple-element.19), channel_id=1, replica_groups=mesh['pipe'=8,'section'=4,'tensor'=8] {'tensor'}, use_global_device_ids=true, to_apply=%region_1.2 | all-reduce | flops 1024 | bytes 8192 | tf_op jit(solution)/shard_map/psum | solution.py:37
  224.6 1.3 fusion.8
  225.8 6.5 %copy.29 = bf16[8,256,1024]{2,1,0:T(8,128)(2,1)} copy(bf16[8,256,1024]{1,2,0:T(8,128)(2,1)} %fusion.10) | data formatting | bytes 8388608 | tf_op jit(solution)/shard_map/rd,bdc->rbc/dot_general | solution.py:40
  232.3 6.8 %fusion.21 = f32[512,2048]{1,0:T(8,128)} fusion(bf16[512,1024]{1,0:T(8,128)(2,1)} %bitcast.51, bf16[2048,1024]{1,0:T(8,128)(2,1)} %bitcast.50), kind=kOutput, calls=%fused_computation.49 | convolution fusion | flops 2147483648 | bytes 9437184 | tf_op jit(solution)/shard_map/rd,bdc->rbc/dot_general | solution.py:40
  239.2 6.3 %convert_bitcast_fusion = bf16[8,1024,256]{2,1,0:T(8,128)(2,1)} fusion(bf16[512,1024,1]{1,0,2:T(8,128)(2,1)} %bitcast.52, bf16[512,8,256]{0,2,1:T(8,128)(2,1)} %bitcast.63), kind=kOutput, calls=%fused_computation.5 | convolution fusion | flops 2149580800 | bytes 7340032 | tf_op jit(solution)/shard_map/rd,rbc->bdc/dot_general | solution.py:51
  245.4 5.0 %gather_fusion.2 = bf16[8,1024,256]{2,1,0:T(8,128)(2,1)} fusion(bf16[8,1024,256]{2,1,0:T(8,128)(2,1)} %convert_bitcast_fusion, s32[1024]{0:T(1024)S(1)} %pad_clamp_fusion), kind=kCustom, calls=%fused_computation.1.clone | custom fusion | bytes 8388640 | tf_op jit(solution)/shard_map/jit(_take)/gather | solution.py:54
  250.4 4.6 %broadcast_select_fusion = bf16[8,1024,256]{2,1,0:T(8,128)(2,1)} fusion(bf16[8,1024,256]{2,1,0:T(8,128)(2,1)} %gather_fusion.2, pred[8]{0:T(512)(128)(4,1)S(1)} %compare_and_fusion), kind=kLoop, calls=%fused_computation.6 | loop fusion | flops 2097152 | bytes 8388616 | tf_op jit(solution)/shard_map/jit(_take)/select_n | solution.py:54
  255.0 7.2 %all-to-all-start = ((bf16[8,1024,256]{2,1,0:T(8,128)(2,1)}), bf16[8,1024,256]{2,1,0:T(8,128)(2,1)}, u32[]{:S(2)}, u32[]{:S(2)}) async-start(bf16[8,1024,256]{2,1,0:T(8,128)(2,1)} %broadcast_select_fusion), calls=%async_computation.1 | async-start | bytes 8388608 | tf_op jit(solution)/shard_map/all_to_all | solution.py:55
  262.3 0.2 reduce-scatter.5.cloned.1.call-start
  262.5 0.7 fusion.17
  263.2 90.4 %all-to-all-done = bf16[8,1024,256]{2,1,0:T(8,128)(2,1)} async-done(((bf16[8,1024,256]{2,1,0:T(8,128)(2,1)}), bf16[8,1024,256]{2,1,0:T(8,128)(2,1)}, u32[]{:S(2)}, u32[]{:S(2)}) %all-to-all-start) | async-done | bytes 4194336 | tf_op jit(solution)/shard_map/all_to_all | solution.py:55
  353.6 4.9 %fusion = f32[4,1024,256]{2,0,1:T(4,128)S(1)} fusion(bf16[8,1024,256]{2,1,0:T(8,128)(2,1)} %all-to-all-done, s32[8]{0:T(128)S(1)} %fusion.17), kind=kOutput, calls=%fused_computation.3 | convolution fusion | flops 16777248 | bytes 8388640 | tf_op jit(solution)/shard_map/lq,qdc->ldc/dot_general | solution.py:60
  358.5 2.7 copy.35
  361.3 1.4 fusion.3
  362.7 1.8 convert_element_type.39
  364.5 52.6 %reduce-scatter.5.cloned.1.call-done = f32[1,1024,256]{2,1,0:T(8,128)} async-done(((f32[4,1024,256]{2,1,0:T(8,128)}), f32[1,1024,256]{2,1,0:T(8,128)}) %reduce-scatter.5.cloned.1.call-update) | async-done | bytes 1048592 | tf_op jit(solution)/shard_map/reduce_scatter | solution.py:61
  417.0 2.1 convert_element_type.45
  (20 shorter events, 0.4 us)
Async XLA Ops:
  7.2 145.7 %all-gather.4.cloned.1.call-start = ((), (), s32[]{:S(2)}) async-start(), calls=%async_computation.3 | async-start | bytes 17301504 | tf_op jit(solution)/shard_map/all_gather | solution.py:24
  7.9 196.6 %all-gather.6.cloned.1.call-start = ((), (), s32[]{:S(2)}) async-start(), calls=%async_computation.5 | async-start | bytes 2359296 | tf_op jit(solution)/shard_map/all_gather | solution.py:46
  9.8 352.9 %reduce-scatter.3.cloned.1.call-start = ((), (), s32[]{:S(2)}) async-start(), calls=%async_computation.4 | async-start | bytes 4718592 | tf_op jit(solution)/shard_map/reduce_scatter | solution.py:43
  171.0 33.5 %copy-start = (bf16[1,1,2,256,1024]{4,3,2,1,0:T(8,128)(2,1)S(1)}, bf16[1,1,2,256,1024]{4,3,2,1,0:T(8,128)(2,1)}, u32[]{:S(2)}) copy-start(bf16[1,1,2,256,1024]{4,3,2,1,0:T(8,128)(2,1)} %param.8) | copy-start | bytes 3145732
  255.0 98.6 %all-to-all-start = ((bf16[8,1024,256]{2,1,0:T(8,128)(2,1)}), bf16[8,1024,256]{2,1,0:T(8,128)(2,1)}, u32[]{:S(2)}, u32[]{:S(2)}) async-start(bf16[8,1024,256]{2,1,0:T(8,128)(2,1)} %broadcast_select_fusion), calls=%async_computation.1 | async-start | bytes 8388608 | tf_op jit(solution)/shard_map/all_to_all | solution.py:55
  262.3 154.8 %reduce-scatter.5.cloned.1.call-start = ((), (), s32[]{:S(2)}) async-start(), calls=%async_computation.6 | async-start | bytes 5242880 | tf_op jit(solution)/shard_map/reduce_scatter | solution.py:61
Sparse Core Ops, SparseCore 0:
  10.8 142.0 all-gather.3
  155.3 49.2 all-gather.5
  239.3 95.7 reduce-scatter.2
  361.4 55.5 reduce-scatter.4
where the time goes:
time: 426 us
  waiting for transfers between devices  260 us (61%)
  blocking collectives  61.5 us (14%)
  local copies, waits for them, and re-layouts  31.4 us (7%)
  other arithmetic  24.2 us (6%)
  matrix products  23.4 us (5%)
  between operations  17.1 us (4%)
  starting transfers between devices  7.58 us (2%)
    all_to_all x1, waiting for transfers between devices, per_device(): lax.all_to_all(outgoing_grads, 'pipe', split_axis=0, concat_axis=0, tiled...  90.4 us
    all_gather x1, waiting for transfers between devices, per_device(): lax.all_gather(held_kv, ('pipe', 'section'), axis=0, tiled=True)  87.9 us
    reduce_scatter x1, waiting for transfers between devices, per_device(): lax.psum_scatter(per_layer, 'section', scatter_dimension=0, tiled=True)  52.6 us
    all_gather x1, blocking collectives, per_device(): lax.all_gather(norm_gain, ('pipe', 'section'), axis=0, tiled=True)  46.9 us
    all_gather x1, waiting for transfers between devices, per_device(): upstream = lax.all_gather(upstream_local, 'tensor', axis=1, tiled=True)  28.8 us
    psum x1, blocking collectives, per_device(): squares = lax.psum(jnp.sum(inputs * inputs, axis=1), 'tensor')  14.6 us
  transfers between devices with their start and end apart: 5, of which 4 were waited for; matrix products, arithmetic and copies ran while one was open for 13% of the time, Pallas kernels for 0%

commit v1 on v0

--- a/solution.py
+++ b/solution.py
@@ -21,7 +21,12 @@
     section_count = lax.axis_size("section")
     layer_index = section_layer[pipe_index, section_index]
     every_block, every_gain = (
-        lax.all_gather(held_kv, ("pipe", "section"), axis=0, tiled=True),
+        jnp.concatenate(
+            lax.all_to_all(
+                jnp.stack([held_kv] * lax.axis_size(("pipe", "section"))), ("pipe", "section"), 0, 0
+            ),
+            axis=0,
+        ),
         lax.all_gather(norm_gain, ("pipe", "section"), axis=0, tiled=True),
     )
     sources = jnp.arange(pipe_count, dtype=jnp.int32) * section_count + layer_index

time: 426 us -> 668 us (1.57)
  blocking collectives: 61.5 us -> 404 us
  waiting for transfers between devices: 260 us -> 143 us
  starting transfers between devices: 7.58 us -> 20.3 us
    all_gather x1, blocking collectives: 46.9 us -> 389 us  [per_device(): lax.all_gather(norm_gain, ('pipe', 'section'), axis=0, tiled=True)]
    all_gather x1 -> x0, waiting for transfers between devices: 87.9 us -> none  [per_device(): lax.all_gather(held_kv, ('pipe', 'section'), axis=0, tiled=True)]
    all_gather x1, waiting for transfers between devices: 28.8 us -> 0.01 us  [per_device(): upstream = lax.all_gather(upstream_local, 'tensor', axis=1, tiled=True)]
    all_to_all x0 -> x1, starting transfers between devices: none -> 13 us  [per_device(): lax.all_to_all(jnp.stack([held_kv] * lax.axis_size(('pipe', 'section'))),...]
    another operation x0 -> x1, local copies, waits for them, and re-layouts: none -> 6.75 us  [per_device(): jnp.stack([held_kv] * lax.axis_size(('pipe', 'section')))]
  transfers between devices with their start and end apart: 5 -> 5, of which waited for: 4 -> 2; matrix products, arithmetic and copies ran while one was open for 13% -> 8% of each run, Pallas kernels for 0% -> 0%
where the time goes in v1:
time: 668 us; the launch traced here: 667 us
  blocking collectives  404 us (60%)
  waiting for transfers between devices  143 us (21%)
  local copies, waits for them, and re-layouts  35.9 us (5%)
  matrix products  23.5 us (4%)
  other arithmetic  23.2 us (3%)
  starting transfers between devices  20.3 us (3%)
  between operations  17.1 us (3%)
    all_gather x1, blocking collectives, per_device(): lax.all_gather(norm_gain, ('pipe', 'section'), axis=0, tiled=True)  389 us
    all_to_all x1, waiting for transfers between devices, per_device(): lax.all_to_all(outgoing_grads, 'pipe', split_axis=0, concat_axis=0, tiled...  91.5 us
    reduce_scatter x1, waiting for transfers between devices, per_device(): lax.psum_scatter(per_layer, 'section', scatter_dimension=0, tiled=True)  51 us
    psum x1, blocking collectives, per_device(): squares = lax.psum(jnp.sum(inputs * inputs, axis=1), 'tensor')  15 us
  transfers between devices with their start and end apart: 5, of which 2 were waited for; matrix products, arithmetic and copies ran while one was open for 8% of the time, Pallas kernels for 0%

profile of v1, /device:TPU:1, one launch (start us, length us, event | category | flops | bytes accessed | tf_op | source)
XLA Modules:
  0.0 666.9 jit_solution(282979921165631776)
XLA Ops:
  7.2 6.8 %stack.2 = bf16[32,1,1024,256]{3,2,1,0:T(8,128)(2,1)} broadcast(bf16[1024,256]{1,0:T(8,128)(2,1)} %bitcast.56), dimensions={2,3} | broadcast | bytes 17301504 | tf_op jit(solution)/shard_map/stack | solution.py:26
  13.9 13.0 %all-to-all-start = ((bf16[32,1,1024,256]{3,2,1,0:T(8,128)(2,1)}), bf16[32,1,1024,256]{3,2,1,0:T(8,128)(2,1)}, u32[]{:S(2)}, u32[]{:S(2)}) async-start(bf16[32,1,1024,256]{3,2,1,0:T(8,128)(2,1)} %stack.2), calls=%async_computation | async-start | bytes 33554432 | tf_op jit(solution)/shard_map/all_to_all | solution.py:25
  27.0 0.8 copy.39
  27.8 0.0 reduce-scatter.3.cloned.1.call-start
  27.9 0.6 dynamic_slice.13
  31.7 0.3 fusion.6
  32.0 389.3 %all-gather = bf16[32,1,1024]{2,1,0:T(2,128)(2,1)S(1)} all-gather(bf16[1,1,1024]{2,1,0:T(2,128)(2,1)S(1)} %bitcast.64), channel_id=1, replica_groups=mesh['pipe'=8,'section'=4,'tensor'=8] {'pipe','section'}, dimensions={0}, use_global_device_ids=true | all-gather | bytes 67584 | tf_op jit(solution)/shard_map/all_gather | solution.py:30
  421.3 0.7 fusion.18
  422.0 0.7 compare_and_fusion.2
  422.6 0.7 compare_and_fusion.1
  423.4 0.1 select_reduce_fusion
  423.5 8.5 %gather_fusion = bf16[8,1024,256]{2,1,0:T(8,128)(2,1)} fusion(bf16[32,1024,256]{2,1,0:T(8,128)(2,1)} %bitcast.6, s32[1024]{0:T(1024)S(1)} %pad_clamp_fusion.2), kind=kCustom, calls=%fused_computation.2 | custom fusion | bytes 8388640 | tf_op jit(solution)/shard_map/jit(_take)/gather | solution.py:33
  432.1 4.6 broadcast_select_fusion.2
  436.7 4.9 gather_fusion.1
  441.6 4.6 fusion.10
  446.2 5.4 fusion.5
  451.6 15.0 %all-reduce = (f32[512]{0:T(512)S(1)}, f32[512]{0:T(512)S(1)}) all-reduce(f32[512]{0:T(512)S(1)} %bitcast.63, f32[512]{0:T(512)S(1)} %get-tuple-element.19), channel_id=1, replica_groups=mesh['pipe'=8,'section'=4,'tensor'=8] {'tensor'}, use_global_device_ids=true, to_apply=%region_1.2 | all-reduce | flops 1024 | bytes 8192 | tf_op jit(solution)/shard_map/psum | solution.py:42
  466.7 1.3 fusion.8
  468.0 6.5 copy.29
  474.5 6.8 %fusion.21 = f32[512,2048]{1,0:T(8,128)} fusion(bf16[512,1024]{1,0:T(8,128)(2,1)} %bitcast.53, bf16[2048,1024]{1,0:T(8,128)(2,1)} %bitcast.52), kind=kOutput, calls=%fused_computation.49 | convolution fusion | flops 2147483648 | bytes 9437184 | tf_op jit(solution)/shard_map/rd,bdc->rbc/dot_general | solution.py:45
  481.3 6.3 convert_bitcast_fusion
  487.6 4.9 gather_fusion.2
  492.6 5.0 broadcast_select_fusion
  497.5 7.1 %all-to-all-start.1 = ((bf16[8,1024,256]{2,1,0:T(8,128)(2,1)}), bf16[8,1024,256]{2,1,0:T(8,128)(2,1)}, u32[]{:S(2)}, u32[]{:S(2)}) async-start(bf16[8,1024,256]{2,1,0:T(8,128)(2,1)} %broadcast_select_fusion), calls=%async_computation.2 | async-start | bytes 8388608 | tf_op jit(solution)/shard_map/all_to_all | solution.py:60
  504.6 0.2 reduce-scatter.5.cloned.1.call-start
  504.8 91.5 %all-to-all-done.1 = bf16[8,1024,256]{2,1,0:T(8,128)(2,1)} async-done(((bf16[8,1024,256]{2,1,0:T(8,128)(2,1)}), bf16[8,1024,256]{2,1,0:T(8,128)(2,1)}, u32[]{:S(2)}, u32[]{:S(2)}) %all-to-all-start.1) | async-done | bytes 4194336 | tf_op jit(solution)/shard_map/all_to_all | solution.py:60
  596.4 4.9 fusion
  601.3 2.7 copy.35
  604.1 1.4 fusion.3
  605.5 1.8 convert_element_type.39
  607.3 51.0 %reduce-scatter.5.cloned.1.call-done = f32[1,1024,256]{2,1,0:T(8,128)} async-done(((f32[4,1024,256]{2,1,0:T(8,128)}), f32[1,1024,256]{2,1,0:T(8,128)}) %reduce-scatter.5.cloned.1.call-update) | async-done | bytes 1048592 | tf_op jit(solution)/shard_map/reduce_scatter | solution.py:66
  658.3 2.1 convert_element_type.45
  (26 shorter events, 0.2 us)
Async XLA Ops:
  13.9 13.0 %copy-start.1 = (bf16[1,1,2,256,256]{4,3,2,1,0:T(8,128)(2,1)S(1)}, bf16[1,1,2,256,256]{4,3,2,1,0:T(8,128)(2,1)}, u32[]{:S(2)}) copy-start(bf16[1,1,2,256,256]{4,3,2,1,0:T(8,128)(2,1)} %param.13) | copy-start | bytes 786436
  13.9 14.0 %copy-start.3 = (s32[8,4]{0,1:T(4,128)S(1)}, s32[8,4]{0,1:T(4,128)}, u32[]{:S(2)}) copy-start(s32[8,4]{0,1:T(4,128)} %param.12) | copy-start | bytes 388
  13.9 17.8 %copy-start = (bf16[1,1,2,256,1024]{4,3,2,1,0:T(8,128)(2,1)S(1)}, bf16[1,1,2,256,1024]{4,3,2,1,0:T(8,128)(2,1)}, u32[]{:S(2)}) copy-start(bf16[1,1,2,256,1024]{4,3,2,1,0:T(8,128)(2,1)} %param.8) | copy-start | bytes 3145732
  13.9 18.1 %copy-start.2 = (bf16[1,1024]{1,0:T(2,128)(2,1)S(1)}, bf16[1,1024]{1,0:T(2,128)(2,1)}, u32[]{:S(2)}) copy-start(bf16[1,1024]{1,0:T(2,128)(2,1)} %param.9) | copy-start | bytes 6148
  13.9 409.6 %all-to-all-start = ((bf16[32,1,1024,256]{3,2,1,0:T(8,128)(2,1)}), bf16[32,1,1024,256]{3,2,1,0:T(8,128)(2,1)}, u32[]{:S(2)}, u32[]{:S(2)}) async-start(bf16[32,1,1024,256]{3,2,1,0:T(8,128)(2,1)} %stack.2), calls=%async_computation | async-start | bytes 33554432 | tf_op jit(solution)/shard_map/all_to_all | solution.py:25
  26.9 419.3 %all-gather.3.cloned.1.call-start = ((), (), s32[]{:S(2)}) async-start(), calls=%async_computation.5 | async-start | bytes 2359296 | tf_op jit(solution)/shard_map/all_gather | solution.py:51
  27.8 577.7 %reduce-scatter.3.cloned.1.call-start = ((), (), s32[]{:S(2)}) async-start(), calls=%async_computation.4 | async-start | bytes 4718592 | tf_op jit(solution)/shard_map/reduce_scatter | solution.py:48
  497.5 98.8 %all-to-all-start.1 = ((bf16[8,1024,256]{2,1,0:T(8,128)(2,1)}), bf16[8,1024,256]{2,1,0:T(8,128)(2,1)}, u32[]{:S(2)}, u32[]{:S(2)}) async-start(bf16[8,1024,256]{2,1,0:T(8,128)(2,1)} %broadcast_select_fusion), calls=%async_computation.2 | async-start | bytes 8388608 | tf_op jit(solution)/shard_map/all_to_all | solution.py:60
  504.6 153.7 %reduce-scatter.5.cloned.1.call-start = ((), (), s32[]{:S(2)}) async-start(), calls=%async_computation.6 | async-start | bytes 5242880 | tf_op jit(solution)/shard_map/reduce_scatter | solution.py:66
Sparse Core Ops, SparseCore 0:
  30.1 126.2 all-gather.2
  481.5 93.9 reduce-scatter.2
  604.2 54.0 reduce-scatter.4
